TPU v7x, 32 devices: a whole 2x2x4 slice. The times are simulated.
32 devices in a mesh: groups: 2 (over y), rows: 16 (over z, x, core).
Axes of the slice: x: 2, y: 2, z: 4, core: 2. Of those that a mesh axis runs over, the one named last changes fastest.
Arguments:
- tile_values: float32 [5120, 128, 128], P(('groups', 'rows')), parts along dimension 0, may hold values from 0.01 to 1
- tile_row: int32 [5120], P(('groups', 'rows')), parts along dimension 0, may hold values from 0 to 127, as said below
- tile_col: int32 [5120], P(('groups', 'rows')), parts along dimension 0, may hold values from 0 to 127, as said below
- row_count: int32 [256], P(('groups', 'rows')), parts along dimension 0, may hold values from 1 to 24, as said below
- start_basis: float32 [24, 32768], P(None, ('groups', 'rows')), parts along dimension 1, may hold values from -6 to 6
Outputs:
- right_basis: float32 [24, 32768], P(None, ('groups', 'rows')), parts along dimension 1
There are 2 independent parts, one for each index of `groups`. A program takes and returns all parts, laid end to end along the dimension named above; each array names one. Nothing has to cross between parts.
Inputs may be any that keep to these rules, and one draw needn't show every extreme that they name: `tile_row`: each device's slots hold its 8 block rows in order, row_count of a row consecutive slots for it, then empty slots that carry the device's last row. `tile_col`: within 16 of the slot's row; each row's slots name its own index once and no index twice; empty slots name their row's own index. `row_count`: the counts of one device's rows sum to at most 160, which some device reaches.
All inputs are finite; a program needn't handle non-finite values.
Results may differ from a plain program's by a relative error of at most 0.0003.
Values sent between devices are 32-bit elements; how exact they have to be, the bound alone decides.
A program may use at most 64 MiB of HBM per device.

v0:
```python
import math

import jax
import jax.numpy as jnp
from jax import lax
from jax.sharding import PartitionSpec as P

ITERS = 2


def shifted(value, axis, steps):
    count = lax.axis_size(axis)
    first, last = (max(0, -steps), min(count, count - steps))
    return lax.ppermute(value, axis, [(source, source + steps) for source in range(first, last)])


def body(tile_values, tile_row, tile_col, row_count, start_basis):
    high = lax.Precision.HIGHEST
    slot_total = tile_values.shape[0]
    tile_len = tile_values.shape[1]
    rows_here = row_count.shape[0]
    vectors = start_basis.shape[0]
    device = lax.axis_index("rows")
    first_row = device * rows_here
    live_slot = (jnp.arange(slot_total) < jnp.sum(row_count)).astype(jnp.float32)
    row_local = tile_row - first_row
    col_local = tile_col - (first_row - 2 * rows_here)
    row_hot = (row_local[:, None] == jnp.arange(rows_here)[None, :]).astype(
        jnp.float32
    ) * live_slot[:, None]
    col_hot = (col_local[:, None] == jnp.arange(5 * rows_here)[None, :]).astype(
        jnp.float32
    ) * live_slot[:, None]
    row_mass = jnp.dot(row_hot.T, jnp.sum(tile_values, axis=2), precision=high)
    col_window = jnp.dot(col_hot.T, jnp.sum(tile_values, axis=1), precision=high).reshape(
        5, rows_here, tile_len
    )
    col_mass = col_window[2]
    for offset in (-2, -1, 1, 2):
        col_mass = col_mass + shifted(col_window[offset + 2], "rows", offset)
    row_scale = 1.0 / jnp.sqrt(row_mass)
    col_scale = 1.0 / jnp.sqrt(col_mass)
    all_mass = lax.psum(jnp.sum(col_mass), "rows")
    unit_vec = jnp.sqrt(col_mass / all_mass).reshape(-1)
    basis_now = start_basis.reshape(vectors, rows_here, tile_len)
    orthonormal = start_basis
    for step in range(ITERS):
        scaled = basis_now * col_scale[None]
        pieces = []
        for offset in (-2, -1, 0, 1, 2):
            if offset == 0:
                pieces.append(scaled)
            else:
                pieces.append(shifted(scaled, "rows", -offset))
        window = jnp.concatenate(pieces, axis=1)
        gathered = jnp.take(window, col_local, axis=1)
        forward = jnp.einsum("sij,ksj->ksi", tile_values, gathered, precision=high)
        image_rows = jnp.einsum("sr,ksi->kri", row_hot, forward, precision=high) * row_scale[None]
        weighted = image_rows * row_scale[None]
        back_prod = jnp.einsum(
            "sij,ksi->ksj", tile_values, jnp.take(weighted, row_local, axis=1), precision=high
        )
        col_terms = jnp.einsum("sc,ksj->kcj", col_hot, back_prod, precision=high).reshape(
            vectors, 5, rows_here, tile_len
        )
        summed = col_terms[:, 2]
        for offset in (-2, -1, 1, 2):
            summed = summed + shifted(col_terms[:, offset + 2], "rows", offset)
        folded = (summed * col_scale[None]).reshape(vectors, rows_here * tile_len)
        along_unit = lax.psum(jnp.dot(folded, unit_vec, precision=high), "rows")
        cleaned = folded - along_unit[:, None] * unit_vec[None, :]
        gram_matrix = lax.psum(jnp.dot(cleaned, cleaned.T, precision=high), "rows")
        factor = jnp.linalg.cholesky(gram_matrix)
        orthonormal = lax.linalg.triangular_solve(factor, cleaned, left_side=True, lower=True)
        basis_now = orthonormal.reshape(vectors, rows_here, tile_len)
    box_total = rows_here * tile_len * lax.axis_size("rows")
    return orthonormal * math.sqrt(box_total)


def solution(mesh):
    placed = (
        P(("groups", "rows"), None, None),
        P(("groups", "rows")),
        P(("groups", "rows")),
        P(("groups", "rows")),
        P(None, ("groups", "rows")),
    )
    return jax.shard_map(
        body, mesh=mesh, in_specs=placed, out_specs=P(None, ("groups", "rows")), check_vma=False
    )
```

profile of v0, /device:TPU:0, one launch (start us, length us, event | category | flops | bytes accessed | tf_op | source)
XLA Modules:
  0.0 364.7 jit_solution(13404329874827476226)
XLA Ops:
  0.0 6.8 %fusion.132 = (f32[160,128]{1,0:T(8,128)S(1)}, f32[160,128]{1,0:T(8,128)S(1)}) fusion(f32[160,128,128]{2,1,0:T(8,128)} %param.12), kind=kLoop, calls=%fused_computation.167 | loop fusion | flops 5201920 | bytes 10649600 | tf_op jit(solution)/shard_map/reduce_sum | solution.py:34
  6.8 0.6 reduce_sum.36
  7.5 0.7 compare_and_fusion.1
  8.1 0.2 fusion.82
  8.3 1.3 collective-permute-start
  9.6 5.5 %collective-permute-start.3 = (f32[8,128]{1,0:T(8,128)S(1)}, f32[8,128]{1,0:T(8,128)S(1)}, u32[]{:S(2)}, u32[]{:S(2)}) collective-permute-start(f32[8,128]{1,0:T(8,128)S(1)} %get-tuple-element.28), channel_id=1, source_target_pairs={{0,2},{1,3},{2,4},{3,5},{4,6},{5,7},{6,8},{7,9},{8,10},{9,11},{10,... | collective-permute-start | bytes 12296 | tf_op jit(solution)/shard_map/ppermute | solution.py:14
  15.1 1.5 collective-permute-start.2
  16.6 1.3 collective-permute-start.1
  17.9 0.2 convolution_rsqrt_fusion
  18.2 4.5 %collective-permute-done.1 = f32[8,128]{1,0:T(8,128)S(1)} collective-permute-done((f32[8,128]{1,0:T(8,128)S(1)}, f32[8,128]{1,0:T(8,128)S(1)}, u32[]{:S(2)}, u32[]{:S(2)}) %collective-permute-start.1) | collective-permute-done | bytes 4128 | tf_op jit(solution)/shard_map/ppermute | solution.py:14
  22.6 0.6 fusion.133
  23.2 32.5 %psum.35 = f32[]{:T(128)} all-reduce(f32[]{:T(128)} %get-tuple-element.10), channel_id=1, replica_groups=mesh['groups'=2,'rows'=16] {'rows'}, use_global_device_ids=true, to_apply=%region_4.7 | all-reduce | flops 1 | bytes 8 | tf_op jit(solution)/shard_map/psum | solution.py:43
  55.7 0.7 divide_sqrt_fusion
  56.4 1.3 collective-permute-start.4
  57.7 1.3 collective-permute-start.7
  59.0 1.3 collective-permute-start.6
  60.3 3.6 collective-permute-start.5
  63.9 0.4 collective-permute-done.5
  64.3 0.9 gather_fusion
  65.2 19.0 %fusion.20 = f32[24,160,128]{2,0,1:T(8,128)S(1)} fusion(f32[160,128,128]{2,1,0:T(8,128)} %param.12, f32[160,24,128]{2,1,0:T(8,128)S(1)} %gather_fusion, pred[160]{0:T(512)(128)(4,1)S(1)} %get-tuple-element.15), kind=kOutput, calls=%fused_computation.24 | convolution fusion | flops 755466240 | bytes 14418080 | tf_op jit(solution)/shard_map/sij,ksj->ksi/dot_general | solution.py:57
  84.2 1.3 fusion.44
  85.5 0.8 gather_fusion.1
  86.4 11.9 %fusion.23 = f32[24,160,128]{2,0,1:T(8,128)S(1)} fusion(f32[160,128,128]{2,1,0:T(8,128)} %param.12, f32[160,24,128]{2,1,0:T(8,128)S(1)} %gather_fusion.1, pred[160]{0:T(512)(128)(4,1)S(1)} %get-tuple-element.13), kind=kOutput, calls=%fused_computation.25 | convolution fusion | flops 755466240 | bytes 14418080 | tf_op jit(solution)/shard_map/sij,ksi->ksj/dot_general | solution.py:60
  98.3 1.3 fusion.32
  99.8 7.2 %collective-permute-start.11 = (f32[24,8,128]{2,0,1:T(8,128)S(1)}, f32[24,8,128]{2,0,1:T(8,128)S(1)}, u32[]{:S(2)}, u32[]{:S(2)}) collective-permute-start(f32[24,8,128]{2,0,1:T(8,128)S(1)} %bitcast.183), channel_id=1, source_target_pairs={{0,2},{1,3},{2,4},{3,5},{4,6},{5,7},{6,8},{7,9},{8,10},{9,11},{10,... | collective-permute-start | bytes 294920 | tf_op jit(solution)/shard_map/ppermute | solution.py:14
  107.0 1.3 collective-permute-start.8
  108.3 1.3 collective-permute-start.9
  109.6 3.0 collective-permute-start.10
  112.6 0.9 collective-permute-done.8
  113.6 0.2 convolution_bitcast_fusion.4
  113.8 32.5 %psum.36 = f32[24]{0:T(128)S(1)} all-reduce(f32[24]{0:T(128)S(1)} %convolution_bitcast_fusion.4), channel_id=1, replica_groups=mesh['groups'=2,'rows'=16] {'rows'}, use_global_device_ids=true, to_apply=%region_5.8 | all-reduce | flops 24 | bytes 192 | tf_op jit(solution)/shard_map/psum | solution.py:70
  146.2 0.3 convolution_bitcast_fusion.2
  146.5 57.6 %psum.37 = f32[24,24]{0,1:T(8,128)S(1)} all-reduce(f32[24,24]{0,1:T(8,128)S(1)} %convolution_bitcast_fusion.2), channel_id=1, replica_groups=mesh['groups'=2,'rows'=16] {'rows'}, use_global_device_ids=true, to_apply=%region_6.0 | all-reduce | flops 576 | bytes 4608 | tf_op jit(solution)/shard_map/psum | solution.py:72
  204.1 0.1 copy.74
  204.2 2.2 cholesky.44
  206.4 0.6 compare_reduce_fusion.1
  207.1 0.6 fusion.101
  207.7 1.8 custom-call.6
  209.6 0.3 convolution_bitcast_fusion
  209.9 1.3 collective-permute-start.12
  211.2 1.3 collective-permute-start.15
  212.5 1.3 collective-permute-start.14
  213.8 3.0 collective-permute-start.13
  216.9 0.9 collective-permute-done.13
  217.9 0.9 gather_fusion.2
  218.7 19.2 %fusion.26 = f32[24,160,128]{2,0,1:T(8,128)S(1)} fusion(f32[160,128,128]{2,1,0:T(8,128)} %param.12, f32[160,24,128]{2,1,0:T(8,128)S(1)} %gather_fusion.2, pred[160]{0:T(512)(128)(4,1)S(1)} %get-tuple-element.15), kind=kOutput, calls=%fused_computation.26 | convolution fusion | flops 755466240 | bytes 14418080 | tf_op jit(solution)/shard_map/sij,ksj->ksi/dot_general | solution.py:57
  238.0 1.3 fusion.53
  239.3 0.8 gather_fusion.3
  240.1 12.0 %fusion.29 = f32[24,160,128]{2,0,1:T(8,128)S(1)} fusion(f32[160,128,128]{2,1,0:T(8,128)} %param.12, f32[160,24,128]{2,1,0:T(8,128)S(1)} %gather_fusion.3, pred[160]{0:T(512)(128)(4,1)S(1)} %get-tuple-element.13), kind=kOutput, calls=%fused_computation.27 | convolution fusion | flops 755466240 | bytes 14418080 | tf_op jit(solution)/shard_map/sij,ksi->ksj/dot_general | solution.py:60
  252.1 1.3 fusion.35
  253.6 7.2 %collective-permute-start.19 = (f32[24,8,128]{2,0,1:T(8,128)S(1)}, f32[24,8,128]{2,0,1:T(8,128)S(1)}, u32[]{:S(2)}, u32[]{:S(2)}) collective-permute-start(f32[24,8,128]{2,0,1:T(8,128)S(1)} %bitcast.184), channel_id=1, source_target_pairs={{0,2},{1,3},{2,4},{3,5},{4,6},{5,7},{6,8},{7,9},{8,10},{9,11},{10,... | collective-permute-start | bytes 294920 | tf_op jit(solution)/shard_map/ppermute | solution.py:14
  260.8 1.3 collective-permute-start.16
  262.1 1.3 collective-permute-start.17
  263.4 3.0 collective-permute-start.18
  266.5 0.9 collective-permute-done.16
  267.4 0.2 convolution_bitcast_fusion.3
  267.6 32.5 %psum.38 = f32[24]{0:T(128)S(1)} all-reduce(f32[24]{0:T(128)S(1)} %convolution_bitcast_fusion.3), channel_id=1, replica_groups=mesh['groups'=2,'rows'=16] {'rows'}, use_global_device_ids=true, to_apply=%region_9.0 | all-reduce | flops 24 | bytes 192 | tf_op jit(solution)/shard_map/psum | solution.py:70
  300.0 0.3 convolution_bitcast_fusion.1
  300.3 57.6 %psum.39 = f32[24,24]{0,1:T(8,128)S(1)} all-reduce(f32[24,24]{0,1:T(8,128)S(1)} %convolution_bitcast_fusion.1), channel_id=1, replica_groups=mesh['groups'=2,'rows'=16] {'rows'}, use_global_device_ids=true, to_apply=%region_10.0 | all-reduce | flops 576 | bytes 4608 | tf_op jit(solution)/shard_map/psum | solution.py:72
  358.1 2.2 cholesky.55
  360.3 0.6 compare_reduce_fusion
  360.9 0.6 fusion.102
  361.6 1.8 custom-call.7
  363.4 1.0 convolution_multiply_fusion
  (60 shorter events, 0.8 us)
Async XLA Ops:
  0.0 56.4 %copy-start = (f32[24,1024]{1,0:T(8,128)S(1)}, f32[24,1024]{1,0:T(8,128)}, u32[]{:S(2)}) copy-start(f32[24,1024]{1,0:T(8,128)} %param.16) | copy-start | bytes 294916
  0.0 6.8 %copy-start.3 = (s32[8]{0:T(128)S(1)}, s32[8]{0:T(128)}, u32[]{:S(2)}) copy-start(s32[8]{0:T(128)} %param.15) | copy-start | bytes 100
  0.0 7.5 %copy-start.2 = (s32[160]{0:T(256)S(1)}, s32[160]{0:T(256)}, u32[]{:S(2)}) copy-start(s32[160]{0:T(256)} %param.14) | copy-start | bytes 1924
  0.0 17.9 %copy-start.1 = (s32[160]{0:T(256)S(1)}, s32[160]{0:T(256)}, u32[]{:S(2)}) copy-start(s32[160]{0:T(256)} %param.13) | copy-start | bytes 1924
  8.3 9.8 %collective-permute-start = (f32[8,128]{1,0:T(8,128)S(1)}, f32[8,128]{1,0:T(8,128)S(1)}, u32[]{:S(2)}, u32[]{:S(2)}) collective-permute-start(f32[8,128]{1,0:T(8,128)S(1)} %get-tuple-element.27), channel_id=1, source_target_pairs={{2,0},{3,1},{4,2},{5,3},{6,4},{7,5},{8,6},{9,7},{10,8},{11,9},{12,... | collective-permute-start | bytes 12296 | tf_op jit(solution)/shard_map/ppermute | solution.py:14
  9.6 8.5 %collective-permute-start.3 = (f32[8,128]{1,0:T(8,128)S(1)}, f32[8,128]{1,0:T(8,128)S(1)}, u32[]{:S(2)}, u32[]{:S(2)}) collective-permute-start(f32[8,128]{1,0:T(8,128)S(1)} %get-tuple-element.28), channel_id=1, source_target_pairs={{0,2},{1,3},{2,4},{3,5},{4,6},{5,7},{6,8},{7,9},{8,10},{9,11},{10,... | collective-permute-start | bytes 12296 | tf_op jit(solution)/shard_map/ppermute | solution.py:14
  15.1 3.0 collective-permute-start.2
  16.6 6.0 %collective-permute-start.1 = (f32[8,128]{1,0:T(8,128)S(1)}, f32[8,128]{1,0:T(8,128)S(1)}, u32[]{:S(2)}, u32[]{:S(2)}) collective-permute-start(f32[8,128]{1,0:T(8,128)S(1)} %get-tuple-element.30), channel_id=1, source_target_pairs={{1,0},{2,1},{3,2},{4,3},{5,4},{6,5},{7,6},{8,7},{9,8},{10,9},{11,1... | collective-permute-start | bytes 12296 | tf_op jit(solution)/shard_map/ppermute | solution.py:14
  56.4 7.5 %collective-permute-start.4 = (f32[24,8,128]{2,0,1:T(8,128)S(1)}, f32[24,8,128]{2,0,1:T(8,128)S(1)}, u32[]{:S(2)}, u32[]{:S(2)}) collective-permute-start(f32[24,8,128]{2,0,1:T(8,128)S(1)} %bitcast_multiply_fusion.1), channel_id=1, source_target_pairs={{0,2},{1,3},{2,4},{3,5},{4,6},{5,7},{6,8},{7,9},{8,10},{9,11},{10,... | collective-permute-start | bytes 294920 | tf_op jit(solution)/shard_map/ppermute | solution.py:14
  57.7 6.6 %collective-permute-start.7 = (f32[24,8,128]{2,0,1:T(8,128)S(1)}, f32[24,8,128]{2,0,1:T(8,128)S(1)}, u32[]{:S(2)}, u32[]{:S(2)}) collective-permute-start(f32[24,8,128]{2,0,1:T(8,128)S(1)} %bitcast_multiply_fusion.1), channel_id=1, source_target_pairs={{2,0},{3,1},{4,2},{5,3},{6,4},{7,5},{8,6},{9,7},{10,8},{11,9},{12,... | collective-permute-start | bytes 294920 | tf_op jit(solution)/shard_map/ppermute | solution.py:14
  59.0 5.3 %collective-permute-start.6 = (f32[24,8,128]{2,0,1:T(8,128)S(1)}, f32[24,8,128]{2,0,1:T(8,128)S(1)}, u32[]{:S(2)}, u32[]{:S(2)}) collective-permute-start(f32[24,8,128]{2,0,1:T(8,128)S(1)} %bitcast_multiply_fusion.1), channel_id=1, source_target_pairs={{1,0},{2,1},{3,2},{4,3},{5,4},{6,5},{7,6},{8,7},{9,8},{10,9},{11,1... | collective-permute-start | bytes 294920 | tf_op jit(solution)/shard_map/ppermute | solution.py:14
  60.3 4.0 %collective-permute-start.5 = (f32[24,8,128]{2,0,1:T(8,128)S(1)}, f32[24,8,128]{2,0,1:T(8,128)S(1)}, u32[]{:S(2)}, u32[]{:S(2)}) collective-permute-start(f32[24,8,128]{2,0,1:T(8,128)S(1)} %bitcast_multiply_fusion.1), channel_id=1, source_target_pairs={{0,1},{1,2},{2,3},{3,4},{4,5},{5,6},{6,7},{7,8},{8,9},{9,10},{10,1... | collective-permute-start | bytes 294920 | tf_op jit(solution)/shard_map/ppermute | solution.py:14
  99.8 12.8 %collective-permute-start.11 = (f32[24,8,128]{2,0,1:T(8,128)S(1)}, f32[24,8,128]{2,0,1:T(8,128)S(1)}, u32[]{:S(2)}, u32[]{:S(2)}) collective-permute-start(f32[24,8,128]{2,0,1:T(8,128)S(1)} %bitcast.183), channel_id=1, source_target_pairs={{0,2},{1,3},{2,4},{3,5},{4,6},{5,7},{6,8},{7,9},{8,10},{9,11},{10,... | collective-permute-start | bytes 294920 | tf_op jit(solution)/shard_map/ppermute | solution.py:14
  107.0 6.5 %collective-permute-start.8 = (f32[24,8,128]{2,0,1:T(8,128)S(1)}, f32[24,8,128]{2,0,1:T(8,128)S(1)}, u32[]{:S(2)}, u32[]{:S(2)}) collective-permute-start(f32[24,8,128]{2,0,1:T(8,128)S(1)} %bitcast.181), channel_id=1, source_target_pairs={{2,0},{3,1},{4,2},{5,3},{6,4},{7,5},{8,6},{9,7},{10,8},{11,9},{12,... | collective-permute-start | bytes 294920 | tf_op jit(solution)/shard_map/ppermute | solution.py:14
  108.3 5.2 %collective-permute-start.9 = (f32[24,8,128]{2,0,1:T(8,128)S(1)}, f32[24,8,128]{2,0,1:T(8,128)S(1)}, u32[]{:S(2)}, u32[]{:S(2)}) collective-permute-start(f32[24,8,128]{2,0,1:T(8,128)S(1)} %bitcast.179), channel_id=1, source_target_pairs={{1,0},{2,1},{3,2},{4,3},{5,4},{6,5},{7,6},{8,7},{9,8},{10,9},{11,1... | collective-permute-start | bytes 294920 | tf_op jit(solution)/shard_map/ppermute | solution.py:14
  109.6 4.0 %collective-permute-start.10 = (f32[24,8,128]{2,0,1:T(8,128)S(1)}, f32[24,8,128]{2,0,1:T(8,128)S(1)}, u32[]{:S(2)}, u32[]{:S(2)}) collective-permute-start(f32[24,8,128]{2,0,1:T(8,128)S(1)} %bitcast.177), channel_id=1, source_target_pairs={{0,1},{1,2},{2,3},{3,4},{4,5},{5,6},{6,7},{7,8},{8,9},{9,10},{10,1... | collective-permute-start | bytes 294920 | tf_op jit(solution)/shard_map/ppermute | solution.py:14
  209.9 6.9 %collective-permute-start.12 = (f32[24,8,128]{2,0,1:T(8,128)S(1)}, f32[24,8,128]{2,0,1:T(8,128)S(1)}, u32[]{:S(2)}, u32[]{:S(2)}) collective-permute-start(f32[24,8,128]{2,0,1:T(8,128)S(1)} %bitcast_multiply_fusion), channel_id=1, source_target_pairs={{0,2},{1,3},{2,4},{3,5},{4,6},{5,7},{6,8},{7,9},{8,10},{9,11},{10,... | collective-permute-start | bytes 294920 | tf_op jit(solution)/shard_map/ppermute | solution.py:14
  211.2 6.6 %collective-permute-start.15 = (f32[24,8,128]{2,0,1:T(8,128)S(1)}, f32[24,8,128]{2,0,1:T(8,128)S(1)}, u32[]{:S(2)}, u32[]{:S(2)}) collective-permute-start(f32[24,8,128]{2,0,1:T(8,128)S(1)} %bitcast_multiply_fusion), channel_id=1, source_target_pairs={{2,0},{3,1},{4,2},{5,3},{6,4},{7,5},{8,6},{9,7},{10,8},{11,9},{12,... | collective-permute-start | bytes 294920 | tf_op jit(solution)/shard_map/ppermute | solution.py:14
  212.5 5.3 %collective-permute-start.14 = (f32[24,8,128]{2,0,1:T(8,128)S(1)}, f32[24,8,128]{2,0,1:T(8,128)S(1)}, u32[]{:S(2)}, u32[]{:S(2)}) collective-permute-start(f32[24,8,128]{2,0,1:T(8,128)S(1)} %bitcast_multiply_fusion), channel_id=1, source_target_pairs={{1,0},{2,1},{3,2},{4,3},{5,4},{6,5},{7,6},{8,7},{9,8},{10,9},{11,1... | collective-permute-start | bytes 294920 | tf_op jit(solution)/shard_map/ppermute | solution.py:14
  213.8 4.0 %collective-permute-start.13 = (f32[24,8,128]{2,0,1:T(8,128)S(1)}, f32[24,8,128]{2,0,1:T(8,128)S(1)}, u32[]{:S(2)}, u32[]{:S(2)}) collective-permute-start(f32[24,8,128]{2,0,1:T(8,128)S(1)} %bitcast_multiply_fusion), channel_id=1, source_target_pairs={{0,1},{1,2},{2,3},{3,4},{4,5},{5,6},{6,7},{7,8},{8,9},{9,10},{10,1... | collective-permute-start | bytes 294920 | tf_op jit(solution)/shard_map/ppermute | solution.py:14
  253.6 12.8 %collective-permute-start.19 = (f32[24,8,128]{2,0,1:T(8,128)S(1)}, f32[24,8,128]{2,0,1:T(8,128)S(1)}, u32[]{:S(2)}, u32[]{:S(2)}) collective-permute-start(f32[24,8,128]{2,0,1:T(8,128)S(1)} %bitcast.184), channel_id=1, source_target_pairs={{0,2},{1,3},{2,4},{3,5},{4,6},{5,7},{6,8},{7,9},{8,10},{9,11},{10,... | collective-permute-start | bytes 294920 | tf_op jit(solution)/shard_map/ppermute | solution.py:14
  260.8 6.5 %collective-permute-start.16 = (f32[24,8,128]{2,0,1:T(8,128)S(1)}, f32[24,8,128]{2,0,1:T(8,128)S(1)}, u32[]{:S(2)}, u32[]{:S(2)}) collective-permute-start(f32[24,8,128]{2,0,1:T(8,128)S(1)} %bitcast.182), channel_id=1, source_target_pairs={{2,0},{3,1},{4,2},{5,3},{6,4},{7,5},{8,6},{9,7},{10,8},{11,9},{12,... | collective-permute-start | bytes 294920 | tf_op jit(solution)/shard_map/ppermute | solution.py:14
  262.1 5.2 %collective-permute-start.17 = (f32[24,8,128]{2,0,1:T(8,128)S(1)}, f32[24,8,128]{2,0,1:T(8,128)S(1)}, u32[]{:S(2)}, u32[]{:S(2)}) collective-permute-start(f32[24,8,128]{2,0,1:T(8,128)S(1)} %bitcast.180), channel_id=1, source_target_pairs={{1,0},{2,1},{3,2},{4,3},{5,4},{6,5},{7,6},{8,7},{9,8},{10,9},{11,1... | collective-permute-start | bytes 294920 | tf_op jit(solution)/shard_map/ppermute | solution.py:14
  263.4 4.0 %collective-permute-start.18 = (f32[24,8,128]{2,0,1:T(8,128)S(1)}, f32[24,8,128]{2,0,1:T(8,128)S(1)}, u32[]{:S(2)}, u32[]{:S(2)}) collective-permute-start(f32[24,8,128]{2,0,1:T(8,128)S(1)} %bitcast.178), channel_id=1, source_target_pairs={{0,1},{1,2},{2,3},{3,4},{4,5},{5,6},{6,7},{7,8},{8,9},{9,10},{10,1... | collective-permute-start | bytes 294920 | tf_op jit(solution)/shard_map/ppermute | solution.py:14
where the time goes:
time: 369 us; the launch traced here: 365 us
  blocking collectives  213 us (58%)
  matrix products  70 us (19%)
  starting transfers between devices  49.4 us (13%)
  other arithmetic  20.2 us (5%)
  waiting for transfers between devices  7.58 us (2%)
  local copies, waits for them, and re-layouts  3.91 us (1%)
    psum x2, blocking collectives, body(): gram_matrix = lax.psum(jnp.dot(cleaned, cleaned.T, precision=high), 'rows')  115 us
    psum x2, blocking collectives, body(): along_unit = lax.psum(jnp.dot(folded, unit_vec, precision=high), 'rows')  64.9 us
    ppermute x20, starting transfers between devices, shifted(): lax.ppermute(value, axis, [(source, source + steps) for source in range(f...  49.4 us
    dot_general x2, matrix products, body(): forward = jnp.einsum('sij,ksj->ksi', tile_values, gathered, precision=high)  38.2 us
    psum x1, blocking collectives, body(): all_mass = lax.psum(jnp.sum(col_mass), 'rows')  32.5 us
    dot_general x2, matrix products, body(): jnp.einsum('sij,ksi->ksj', tile_values, jnp.take(weighted, row_local, axi...  24 us
    ppermute x20, waiting for transfers between devices, shifted(): lax.ppermute(value, axis, [(source, source + steps) for source in range(f...  7.58 us
  transfers between devices with their start and end apart: 20, of which 7 were waited for; matrix products, arithmetic and copies ran while one was open for 0% of the time, Pallas kernels for 0%

commit v1 on v0

v1 whole, which is shorter than its diff:
```python
import functools
import math

import jax
import jax.numpy as jnp
from jax import lax
from jax.experimental import pallas as pl
from jax.experimental.pallas import tpu as pltpu
from jax.sharding import PartitionSpec as P

MOST_ROW = 24
MESH = pl.DeviceIdType.MESH
OFFSETS = (-2, -1, 1, 2)
HIGH = lax.Precision.HIGHEST
NT = (((1,), (1,)), ((), ()))
NN = (((1,), (0,)), ((), ()))
F32 = jnp.float32
BF16 = jnp.bfloat16


def split(value):
    hi = value.astype(BF16).astype(F32)
    return hi, value - hi


def kernel(
    count, near, slots, rows, vectors, tlen, chunks,
    tab, basis, tiles_hbm, out,
    tiles, t_hi, t_lo, c_part, prod, v_win, v_win2, s_win, lhs_win, lhs_row,
    colw, col_in, z_part, z_in, z_own, zext, ar_out, ar_in,
    tile_sem, x_send, x_recv, a_send, a_recv,
):
    me = lax.axis_index("rows")
    far = count // near
    win = 5 * rows
    half = vectors + 8
    col_at, row_at = 0, slots
    cmap_at = 2 * slots
    rmap_at = cmap_at + win * rows
    per = slots // chunks

    tile_copies = []
    for c in range(chunks):
        part = pl.ds(c * per, per)
        copy = pltpu.make_async_copy(tiles_hbm.at[part], tiles.at[part], tile_sem.at[c])
        copy.start()
        tile_copies.append(copy)

    valid = [jnp.logical_and(me + d >= 0, me + d < count) for d in OFFSETS]
    stage_pos = (me % near, me // near)
    stage_len = (near, far)

    def partner(stage, j):
        if stage == 0:
            return (me // near) * near + (me % near + j) % near
        return ((me // near + j) % far) * near + me % near

    barrier = pltpu.get_barrier_semaphore()
    greeted = jnp.int32(near - 1 + far - 1)
    for d, ok in zip(OFFSETS, valid):
        greeted = greeted + ok.astype(jnp.int32)

        @pl.when(ok)
        def _(d=d):
            pl.semaphore_signal(barrier, inc=1, device_id={"rows": me + d}, device_id_type=MESH)

    for stage in (0, 1):
        for j in range(1, stage_len[stage]):
            pl.semaphore_signal(
                barrier, inc=1, device_id={"rows": partner(stage, j)}, device_id_type=MESH
            )

    for b in range(rows):
        v_win[2 * rows + b] = basis[:, b * tlen : (b + 1) * tlen]
    c_part[slots] = jnp.zeros((8, tlen), F32)
    prod[slots] = jnp.zeros((half, tlen), F32)
    zext[...] = jnp.zeros_like(zext)

    def neighbour(which, i, source, target):
        return pltpu.make_async_remote_copy(
            src_ref=source(OFFSETS[i]),
            dst_ref=target(OFFSETS[i]),
            send_sem=x_send.at[which, i],
            recv_sem=x_recv.at[which, i],
            device_id={"rows": me + OFFSETS[i]},
            device_id_type=MESH,
        )

    def send(which, source, target):
        for i in (0, 3, 1, 2):
            @pl.when(valid[i])
            def _(i=i):
                neighbour(which, i, source, target).start()

    def finish(which, source, target):
        for i in range(4):
            @pl.when(valid[i])
            def _(i=i):
                neighbour(which, i, source, target).wait_send()

            @pl.when(valid[3 - i])
            def _(i=i):
                neighbour(which, i, source, target).wait_recv()

    def own_v(d):
        return v_win.at[pl.ds(2 * rows, rows)]

    def to_v(d):
        return v_win.at[pl.ds((2 - d) * rows, rows)]

    def own_v2(d):
        return v_win2.at[pl.ds(2 * rows, rows)]

    def to_v2(d):
        return v_win2.at[pl.ds((2 - d) * rows, rows)]

    def own_s(d):
        return s_win.at[pl.ds(2 * rows, rows)]

    def to_s(d):
        return s_win.at[pl.ds((2 - d) * rows, rows)]

    def part_c(d):
        return colw.at[2 + d]

    def to_c(d):
        return col_in.at[OFFSETS.index(d)]

    def mass_chunk(c):
        tile_copies[c].wait()

        @pl.loop(c * per, (c + 1) * per, unroll=4)
        def _(s):
            tile = tiles[s]
            hi = tile.astype(BF16)
            t_hi[s] = hi
            t_lo[s] = (tile - hi.astype(F32)).astype(BF16)
            c_part[s] = jnp.sum(tile.reshape(tlen // 8, 8, tlen), axis=0)

    mass_chunk(0)
    pl.semaphore_wait(barrier, greeted)
    send(0, own_v, to_v)
    for c in range(1, chunks):
        mass_chunk(c)

    @pl.loop(0, 5)
    def _(w):
        lines = []
        for b in range(rows):
            at = cmap_at + (w * rows + b) * rows
            total = c_part[tab[at]]
            for r in range(1, rows):
                total = total + c_part[tab[at + r]]
            lines.append(jnp.sum(total, axis=0, keepdims=True))
        colw[w] = jnp.concatenate(lines, axis=0)

    send(1, part_c, to_c)
    finish(1, part_c, to_c)
    for i in range(4):
        @pl.when(valid[3 - i])
        def _(i=i):
            colw[2] = colw[2] + col_in[i]

    mass = colw[2]
    col_scale = 1.0 / jnp.sqrt(mass)
    root = jnp.sqrt(mass)
    s_win[2 * rows : 3 * rows] = col_scale
    send(2, own_s, to_s)

    for b in range(rows):
        zext[vectors : vectors + 1, b * tlen : (b + 1) * tlen] = root[b : b + 1]

    def reduce_copy(which, stage, j):
        return pltpu.make_async_remote_copy(
            src_ref=ar_out.at[which, stage],
            dst_ref=ar_in.at[which, stage, j - 1],
            send_sem=a_send.at[which, stage, j - 1],
            recv_sem=a_recv.at[which, stage, j - 1],
            device_id={"rows": partner(stage, j)},
            device_id_type=MESH,
        )

    def reduce_send(which, stage, value):
        ar_out[which, stage] = value
        for j in range(1, stage_len[stage]):
            reduce_copy(which, stage, j).start()

    def reduce_wait(which, stage):
        total = ar_out[which, stage]
        for j in range(1, stage_len[stage]):
            copy = reduce_copy(which, stage, j)
            copy.wait_send()
            copy.wait_recv()
            total = total + ar_in[which, stage, j - 1]
        return total

    def gram_packed():
        value = zext[...]
        gram = lax.dot_general(value[0:32], value, NT, precision=HIGH, preferred_element_type=F32)
        packed = gram[0:8]
        for b in range(1, 4):
            packed = packed + pltpu.roll(gram[8 * b : 8 * b + 8], 32 * b, 1)
        return packed

    lane = lax.broadcasted_iota(jnp.int32, (vectors, 128), 1)
    line = lax.broadcasted_iota(jnp.int32, (vectors, 128), 0)

    def unpack(packed):
        parts = [packed] + [pltpu.roll(packed, 128 - 32 * b, 1) for b in (1, 2)]
        gram = jnp.concatenate(parts, axis=0)
        last = pltpu.roll(packed, 32, 1)
        unit_row = last[0:1]
        mass_all = last[0:1, vectors : vectors + 1]
        along = gram[:, vectors : vectors + 1] / mass_all
        return gram, unit_row, along

    def inverse_factor(gram, unit_row, along):
        work = jnp.where(lane < vectors, gram - along * unit_row, 0.0)
        work = jnp.where(lane == line + 32, 1.0, work)
        for j in range(vectors):
            top = work[j : j + 1]
            ratio = work[:, j : j + 1] / top[:, j : j + 1]
            work = work - jnp.where(line[:, 0:1] > j, ratio, 0.0) * top
        diag = jnp.sum(jnp.where(lane == line, work, 0.0), axis=1, keepdims=True)
        work = work * (1.0 / jnp.sqrt(diag))
        return jnp.where(lane < vectors, pltpu.roll(work, 96, 1), 0.0)

    def mix(factor, value):
        padded = jnp.concatenate([value, jnp.zeros((128 - vectors, tlen), F32)], axis=0)
        return lax.dot_general(factor, padded, NN, precision=HIGH, preferred_element_type=F32)

    for b in range(rows):
        zext[0:vectors, b * tlen : (b + 1) * tlen] = v_win[2 * rows + b]
    reduce_send(0, 0, gram_packed())

    ones8 = jnp.ones((8, tlen), F32)
    zeros8 = jnp.zeros((8, tlen), F32)

    def left_side(value, extra):
        hi, lo = split(value)
        return jnp.concatenate([hi, extra, lo, zeros8], axis=0).astype(BF16)

    def forward():
        @pl.loop(0, slots, unroll=8)
        def _(s):
            left = lhs_win[tab[col_at + s]]
            big = lax.dot_general(left, t_hi[s], NT, preferred_element_type=F32)
            small = lax.dot_general(left[0:half], t_lo[s], NT, preferred_element_type=F32)
            prod[s] = big[0:half] + big[half:] + small

    def row_total(r):
        at = rmap_at + r * MOST_ROW
        total = prod[tab[at]]
        for p in range(1, MOST_ROW):
            total = total + prod[tab[at + p]]
        return total[0:vectors] * (1.0 / total[vectors : vectors + 1])

    def backward(step):
        @pl.loop(0, slots, unroll=8)
        def _(s):
            left = lhs_row[tab[row_at + s]]
            big = lax.dot_general(left, t_hi[s], NN, preferred_element_type=F32)
            small = lax.dot_general(left[0:half], t_lo[s], NN, preferred_element_type=F32)
            prod[s] = big[0:half] + big[half:] + small

        @pl.loop(0, win)
        def _(c):
            at = cmap_at + c * rows
            total = prod[tab[at], 0:vectors]
            for r in range(1, rows):
                total = total + prod[tab[at + r], 0:vectors]
            z_part[step, c] = total

    def exchange_z(step):
        def source(d):
            return z_part.at[step, pl.ds((2 + d) * rows, rows)]

        def target(d):
            return z_in.at[step, OFFSETS.index(d)]

        send(3 + step, source, target)
        finish(3 + step, source, target)
        z_own[...] = z_part[step, 2 * rows : 3 * rows]
        for i in range(4):
            @pl.when(valid[3 - i])
            def _(i=i):
                z_own[...] = z_own[...] + z_in[step, i]

    finish(0, own_v, to_v)
    finish(2, own_s, to_s)

    @pl.loop(0, win, unroll=4)
    def _(c):
        lhs_win[c] = left_side(v_win[c] * s_win[pl.ds(c, 1)], ones8)

    forward()
    reduce_send(0, 1, reduce_wait(0, 0))

    @pl.loop(0, rows)
    def _(r):
        lhs_row[r] = left_side(row_total(r), zeros8)

    backward(0)
    _, _, along = unpack(reduce_wait(0, 1))
    exchange_z(0)
    for b in range(rows):
        cleaned = z_own[b] * col_scale[b : b + 1] - along * root[b : b + 1]
        zext[0:vectors, b * tlen : (b + 1) * tlen] = cleaned
        v_win2[2 * rows + b] = cleaned * col_scale[b : b + 1]
    send(5, own_v2, to_v2)
    reduce_send(1, 0, gram_packed())
    finish(5, own_v2, to_v2)

    @pl.loop(0, win, unroll=4)
    def _(c):
        lhs_win[c] = left_side(v_win2[c], ones8)

    reduce_send(1, 1, reduce_wait(1, 0))
    forward()
    factor = inverse_factor(*unpack(reduce_wait(1, 1)))

    @pl.loop(0, rows)
    def _(r):
        lhs_row[r] = left_side(mix(factor, row_total(r)), zeros8)

    backward(1)
    exchange_z(1)
    for b in range(rows):
        zext[0:vectors, b * tlen : (b + 1) * tlen] = z_own[b] * col_scale[b : b + 1]
    reduce_send(2, 0, gram_packed())
    reduce_send(2, 1, reduce_wait(2, 0))
    gram, unit_row, along = unpack(reduce_wait(2, 1))
    factor = inverse_factor(gram, unit_row, along)
    factor = factor * math.sqrt(count * rows * tlen)
    for b in range(rows):
        cols = slice(b * tlen, (b + 1) * tlen)
        out[:, cols] = mix(factor, zext[0:vectors, cols] - along * root[b : b + 1])


def body(tile_values, tile_row, tile_col, row_count, start_basis):
    slots, tlen = tile_values.shape[:2]
    rows = row_count.shape[0]
    vectors = start_basis.shape[0]
    count = lax.axis_size("rows")
    near = 4 if count <= 16 else 8
    win = 5 * rows
    first = lax.axis_index("rows") * rows
    row_here = tile_row - first
    col_here = tile_col - (first - 2 * rows)
    slot = jnp.arange(slots, dtype=jnp.int32)
    live = slot < jnp.sum(row_count)
    place = jnp.where(live, col_here * rows + row_here, -1)
    cells = jnp.arange(win * rows, dtype=jnp.int32)
    col_map = jnp.min(jnp.where(place[None, :] == cells[:, None], slot[None, :], slots), axis=1)
    line = jnp.arange(rows, dtype=jnp.int32)
    starts = jnp.sum(jnp.where(line[None, :] < line[:, None], row_count[None, :], 0), axis=1)
    spot = jnp.arange(MOST_ROW, dtype=jnp.int32)
    row_map = jnp.where(
        spot[None, :] < row_count[:, None], starts[:, None] + spot[None, :], slots
    ).reshape(-1)
    table = jnp.concatenate([col_here, row_here, col_map, row_map]).astype(jnp.int32)
    chunks = 8
    most = max(near, count // near)
    half = vectors + 8
    vmem = pltpu.VMEM
    return pl.pallas_call(
        functools.partial(kernel, count, near, slots, rows, vectors, tlen, chunks),
        out_shape=jax.ShapeDtypeStruct(start_basis.shape, F32),
        in_specs=[
            pl.BlockSpec(memory_space=pltpu.SMEM),
            pl.BlockSpec(memory_space=pltpu.VMEM),
            pl.BlockSpec(memory_space=pl.ANY),
        ],
        out_specs=pl.BlockSpec(memory_space=pltpu.VMEM),
        scratch_shapes=[
            vmem((slots, tlen, tlen), F32),
            vmem((slots, tlen, tlen), BF16),
            vmem((slots, tlen, tlen), BF16),
            vmem((slots + 1, 8, tlen), F32),
            vmem((slots + 1, half, tlen), F32),
            vmem((win, vectors, tlen), F32),
            vmem((win, vectors, tlen), F32),
            vmem((win, tlen), F32),
            vmem((win, 2 * half, tlen), BF16),
            vmem((rows, 2 * half, tlen), BF16),
            vmem((5, rows, tlen), F32),
            vmem((4, rows, tlen), F32),
            vmem((2, win, vectors, tlen), F32),
            vmem((2, 4, rows, vectors, tlen), F32),
            vmem((rows, vectors, tlen), F32),
            vmem((128, rows * tlen), F32),
            vmem((3, 2, 8, 128), F32),
            vmem((3, 2, most, 8, 128), F32),
            pltpu.SemaphoreType.DMA((chunks,)),
            pltpu.SemaphoreType.DMA((6, 4)),
            pltpu.SemaphoreType.DMA((6, 4)),
            pltpu.SemaphoreType.DMA((3, 2, most)),
            pltpu.SemaphoreType.DMA((3, 2, most)),
        ],
        compiler_params=pltpu.CompilerParams(
            collective_id=0, has_side_effects=True, vmem_limit_bytes=48 * 1024 * 1024
        ),
    )(table, start_basis, tile_values)


def solution(mesh):
    placed = (
        P(("groups", "rows"), None, None),
        P(("groups", "rows")),
        P(("groups", "rows")),
        P(("groups", "rows")),
        P(None, ("groups", "rows")),
    )
    return jax.shard_map(
        body, mesh=mesh, in_specs=placed, out_specs=P(None, ("groups", "rows")), check_vma=False
    )
```

time: 369 us -> 89.5 us (0.24); the launches traced: 365 us -> 89.3 us
  blocking collectives: 213 us -> 0 us
  Pallas kernels: 0 us -> 83.3 us
  matrix products: 70 us -> 0 us
  starting transfers between devices: 49.4 us -> 0 us
  other arithmetic: 20.2 us -> 4.33 us
  waiting for transfers between devices: 7.58 us -> 0 us
    psum x5 -> x0, blocking collectives: 213 us -> none  [the longest x2 115 us: body(): gram_matrix = lax.psum(jnp.dot(cleaned, cleaned.T, precision=high), 'rows')]
    pallas_call x0 -> x1, Pallas kernels: none -> 83.3 us  [body(): pl.pallas_call(functools.partial(kernel, count, near, slots, rows, vector...]
    dot_general x14 -> x0, matrix products: 68.6 us -> none  [the longest x2 38.2 us: body(): forward = jnp.einsum('sij,ksj->ksi', tile_values, gathered, precision=high)]
    ppermute x20 -> x0, starting transfers between devices: 49.4 us -> none  [shifted(): lax.ppermute(value, axis, [(source, source + steps) for source in range(f...]
    another operation x10 -> x0, other arithmetic: 10.7 us -> none  [the longest x6 5.72 us: body(): factor = jnp.linalg.cholesky(gram_matrix)]
    ppermute x20 -> x0, waiting for transfers between devices: 7.58 us -> none  [shifted(): lax.ppermute(value, axis, [(source, source + steps) for source in range(f...]
    reduce_sum x3 -> x2, other arithmetic: 8.02 us -> 2.06 us  [the longest x1 1.29 us: body(): live = slot < jnp.sum(row_count)]
  transfers between devices with their start and end apart: 20 -> 0, of which waited for: 7 -> 0; matrix products, arithmetic and copies ran while one was open for 0% -> 0% of each run, Pallas kernels for 0% -> 0%
where the time goes in v1:
time: 89.5 us; the launch traced here: 89.3 us
  Pallas kernels  83.3 us (93%)
  other arithmetic  4.33 us (5%)
  local copies, waits for them, and re-layouts  1.62 us (2%)
    pallas_call x1, Pallas kernels, body(): pl.pallas_call(functools.partial(kernel, count, near, slots, rows, vector...  83.3 us

profile of v1, /device:TPU:0, one launch (start us, length us, event | category | flops | bytes accessed | tf_op | source)
XLA Modules:
  0.0 89.3 jit_solution(16713232243090650601)
XLA Ops:
  0.0 1.3 %reduce_sum.18 = s32[]{:T(128)} reduce(s32[8]{0:T(128)} %param.8, s32[]{:T(128)} %constant.3.clone.1), dimensions={0}, to_apply=%region_0.0 | reduce | flops 7 | bytes 40 | tf_op jit(solution)/shard_map/reduce_sum | solution.py:351
  1.3 0.8 select_reduce_fusion.1
  2.1 1.3 %compare_select_fusion = (s32[160]{0:T(256)S(1)}, s32[160]{0:T(256)S(1)}, s32[160]{0:T(256)S(1)}) fusion(s32[]{:T(128)} %reduce_sum.18, s32[160]{0:T(256)} %param.7, s32[]{:T(128)S(6)} %sub.15, s32[160]{0:T(256)} %param.6, s32[]{:T(128)S(6)} %mul.9), kind=kLoop, calls=%fused_computation.7 | loop fusion | flops 960 | bytes 3212 | tf_op jit(solution)/shard_map/jit(_where)/select_n | solution.py:352
  3.4 0.1 select_reduce_fusion
  3.5 0.7 add_select_fusion
  4.3 0.1 select_n.24
  4.3 0.1 pad_add_fusion.tab
  4.4 0.0 copy-start
  4.4 0.9 %copy-done = f32[24,1024]{1,0:T(8,128)S(1)} copy-done((f32[24,1024]{1,0:T(8,128)S(1)}, f32[24,1024]{1,0:T(8,128)}, u32[]{:S(2)}) %copy-start) | copy-done | bytes 98328
  5.3 83.3 %shard_map.55 = f32[24,1024]{1,0:T(8,128)S(1)} custom-call(s32[832]{0:T(1024)S(1)} %pad_add_fusion.tab, f32[24,1024]{1,0:T(8,128)S(1)} %copy-done, f32[160,128,128]{2,1,0:T(8,128)} %tiles_hbm.1), custom_call_target="tpu_custom_call" | custom-call | tf_op jit(solution)/shard_map/pallas_call | solution.py:366
  88.6 0.6 copy.7
Async XLA Ops:
  4.4 0.9 %copy-start = (f32[24,1024]{1,0:T(8,128)S(1)}, f32[24,1024]{1,0:T(8,128)}, u32[]{:S(2)}) copy-start(f32[24,1024]{1,0:T(8,128)} %basis.1) | copy-start | bytes 294916

commit v2 on v1

--- a/solution.py
+++ b/solution.py
@@ -26,8 +26,8 @@
 def kernel(
     count, near, slots, rows, vectors, tlen, chunks,
     tab, basis, tiles_hbm, out,
-    tiles, t_hi, t_lo, c_part, prod, v_win, v_win2, s_win, lhs_win, lhs_row,
-    colw, col_in, z_part, z_in, z_own, zext, ar_out, ar_in,
+    tiles, t_own, t_flip, c_part, prod, v_win, v_win2, s_win, lhs_win, lhs_row,
+    row_inv, colw, col_in, z_part, z_in, z_own, zext, ar_out, ar_in,
     tile_sem, x_send, x_recv, a_send, a_recv,
 ):
     me = lax.axis_index("rows")
@@ -133,8 +133,8 @@
         def _(s):
             tile = tiles[s]
             hi = tile.astype(BF16)
-            t_hi[s] = hi
-            t_lo[s] = (tile - hi.astype(F32)).astype(BF16)
+            t_own[s, 0:tlen] = hi
+            t_own[s, tlen:] = (tile - hi.astype(F32)).astype(BF16)
             c_part[s] = jnp.sum(tile.reshape(tlen // 8, 8, tlen), axis=0)
 
     mass_chunk(0)
@@ -154,7 +154,14 @@
             lines.append(jnp.sum(total, axis=0, keepdims=True))
         colw[w] = jnp.concatenate(lines, axis=0)
 
+    def flip(begin, end):
+        @pl.loop(begin, end, unroll=4)
+        def _(s):
+            t_flip[s, 0:tlen] = t_own[s, 0:tlen].T
+            t_flip[s, tlen:] = t_own[s, tlen:].T
+
     send(1, part_c, to_c)
+    flip(0, slots // 2)
     finish(1, part_c, to_c)
     for i in range(4):
         @pl.when(valid[3 - i])
@@ -233,35 +240,43 @@
         zext[0:vectors, b * tlen : (b + 1) * tlen] = v_win[2 * rows + b]
     reduce_send(0, 0, gram_packed())
 
-    ones8 = jnp.ones((8, tlen), F32)
-    zeros8 = jnp.zeros((8, tlen), F32)
-
-    def left_side(value, extra):
+    def left_side(value):
         hi, lo = split(value)
-        return jnp.concatenate([hi, extra, lo, zeros8], axis=0).astype(BF16)
-
-    def forward():
-        @pl.loop(0, slots, unroll=8)
+        return jnp.concatenate(
+            [
+                jnp.concatenate([hi, hi], axis=1),
+                jnp.concatenate([lo, jnp.zeros_like(lo)], axis=1),
+            ],
+            axis=0,
+        ).astype(BF16)
+
+    def forward(step):
+        used = 2 * half if step == 0 else 2 * vectors
+
+        @pl.loop(0, slots, unroll=16)
         def _(s):
-            left = lhs_win[tab[col_at + s]]
-            big = lax.dot_general(left, t_hi[s], NT, preferred_element_type=F32)
-            small = lax.dot_general(left[0:half], t_lo[s], NT, preferred_element_type=F32)
-            prod[s] = big[0:half] + big[half:] + small
-
-    def row_total(r):
+            left = lhs_win[tab[col_at + s], 0:used]
+            both = lax.dot_general(left, t_flip[s], NN, preferred_element_type=F32)
+            prod[s, 0:vectors] = both[0:vectors] + both[vectors : 2 * vectors]
+            if step == 0:
+                prod[s, vectors:] = both[2 * vectors : 2 * vectors + 8]
+
+    def row_total(r, step):
         at = rmap_at + r * MOST_ROW
-        total = prod[tab[at]]
+        used = half if step == 0 else vectors
+        total = prod[tab[at], 0:used]
         for p in range(1, MOST_ROW):
-            total = total + prod[tab[at + p]]
-        return total[0:vectors] * (1.0 / total[vectors : vectors + 1])
+            total = total + prod[tab[at + p], 0:used]
+        if step == 0:
+            row_inv[r] = 1.0 / total[vectors:]
+        return total[0:vectors] * row_inv[r, 0:1]
 
     def backward(step):
-        @pl.loop(0, slots, unroll=8)
+        @pl.loop(0, slots, unroll=16)
         def _(s):
             left = lhs_row[tab[row_at + s]]
-            big = lax.dot_general(left, t_hi[s], NN, preferred_element_type=F32)
-            small = lax.dot_general(left[0:half], t_lo[s], NN, preferred_element_type=F32)
-            prod[s] = big[0:half] + big[half:] + small
+            both = lax.dot_general(left, t_own[s], NN, preferred_element_type=F32)
+            prod[s, 0:vectors] = both[0:vectors] + both[vectors:]
 
         @pl.loop(0, win)
         def _(c):
@@ -286,19 +301,23 @@
             def _(i=i):
                 z_own[...] = z_own[...] + z_in[step, i]
 
+    flip(slots // 2, slots)
+    tail = lax.broadcasted_iota(jnp.int32, (16, 2 * tlen), 0)
+    ones = jnp.where(tail < 8, 1.0, 0.0).astype(BF16)
     finish(0, own_v, to_v)
     finish(2, own_s, to_s)
 
     @pl.loop(0, win, unroll=4)
     def _(c):
-        lhs_win[c] = left_side(v_win[c] * s_win[pl.ds(c, 1)], ones8)
-
-    forward()
+        lhs_win[c, 0 : 2 * vectors] = left_side(v_win[c] * s_win[pl.ds(c, 1)])
+        lhs_win[c, 2 * vectors :] = ones
+
+    forward(0)
     reduce_send(0, 1, reduce_wait(0, 0))
 
     @pl.loop(0, rows)
     def _(r):
-        lhs_row[r] = left_side(row_total(r), zeros8)
+        lhs_row[r] = left_side(row_total(r, 0))
 
     backward(0)
     _, _, along = unpack(reduce_wait(0, 1))
@@ -313,15 +332,15 @@
 
     @pl.loop(0, win, unroll=4)
     def _(c):
-        lhs_win[c] = left_side(v_win2[c], ones8)
+        lhs_win[c, 0 : 2 * vectors] = left_side(v_win2[c])
 
     reduce_send(1, 1, reduce_wait(1, 0))
-    forward()
+    forward(1)
     factor = inverse_factor(*unpack(reduce_wait(1, 1)))
 
     @pl.loop(0, rows)
     def _(r):
-        lhs_row[r] = left_side(mix(factor, row_total(r)), zeros8)
+        lhs_row[r] = left_side(mix(factor, row_total(r, 1)))
 
     backward(1)
     exchange_z(1)
@@ -335,6 +354,33 @@
     for b in range(rows):
         cols = slice(b * tlen, (b + 1) * tlen)
         out[:, cols] = mix(factor, zext[0:vectors, cols] - along * root[b : b + 1])
+
+
+def table_kernel(slots, rows, tile_row, tile_col, row_count, tab):
+    first = lax.axis_index("rows") * rows
+    win = 5 * rows
+    cmap_at = 2 * slots
+    rmap_at = cmap_at + win * rows
+
+    @pl.loop(0, win * rows, unroll=16)
+    def _(i):
+        tab[cmap_at + i] = slots
+
+    start = jnp.int32(0)
+    for r in range(rows):
+        size = row_count[r]
+        for p in range(MOST_ROW):
+            tab[rmap_at + r * MOST_ROW + p] = jnp.where(p < size, start + p, slots)
+        start = start + size
+
+    @pl.loop(0, slots, unroll=8)
+    def _(s):
+        tab[s] = tile_col[s] - (first - 2 * rows)
+        tab[slots + s] = tile_row[s] - first
+
+    @pl.loop(0, start)
+    def _(s):
+        tab[cmap_at + tab[s] * rows + tab[slots + s]] = s
 
 
 def body(tile_values, tile_row, tile_col, row_count, start_basis):
@@ -344,21 +390,13 @@
     count = lax.axis_size("rows")
     near = 4 if count <= 16 else 8
     win = 5 * rows
-    first = lax.axis_index("rows") * rows
-    row_here = tile_row - first
-    col_here = tile_col - (first - 2 * rows)
-    slot = jnp.arange(slots, dtype=jnp.int32)
-    live = slot < jnp.sum(row_count)
-    place = jnp.where(live, col_here * rows + row_here, -1)
-    cells = jnp.arange(win * rows, dtype=jnp.int32)
-    col_map = jnp.min(jnp.where(place[None, :] == cells[:, None], slot[None, :], slots), axis=1)
-    line = jnp.arange(rows, dtype=jnp.int32)
-    starts = jnp.sum(jnp.where(line[None, :] < line[:, None], row_count[None, :], 0), axis=1)
-    spot = jnp.arange(MOST_ROW, dtype=jnp.int32)
-    row_map = jnp.where(
-        spot[None, :] < row_count[:, None], starts[:, None] + spot[None, :], slots
-    ).reshape(-1)
-    table = jnp.concatenate([col_here, row_here, col_map, row_map]).astype(jnp.int32)
+    smem = pl.BlockSpec(memory_space=pltpu.SMEM)
+    table = pl.pallas_call(
+        functools.partial(table_kernel, slots, rows),
+        out_shape=jax.ShapeDtypeStruct((2 * slots + win * rows + rows * MOST_ROW,), jnp.int32),
+        in_specs=[smem] * 3,
+        out_specs=smem,
+    )(tile_row, tile_col, row_count)
     chunks = 8
     most = max(near, count // near)
     half = vectors + 8
@@ -374,15 +412,16 @@
         out_specs=pl.BlockSpec(memory_space=pltpu.VMEM),
         scratch_shapes=[
             vmem((slots, tlen, tlen), F32),
-            vmem((slots, tlen, tlen), BF16),
-            vmem((slots, tlen, tlen), BF16),
+            vmem((slots, 2 * tlen, tlen), BF16),
+            vmem((slots, 2 * tlen, tlen), BF16),
             vmem((slots + 1, 8, tlen), F32),
             vmem((slots + 1, half, tlen), F32),
             vmem((win, vectors, tlen), F32),
             vmem((win, vectors, tlen), F32),
             vmem((win, tlen), F32),
-            vmem((win, 2 * half, tlen), BF16),
-            vmem((rows, 2 * half, tlen), BF16),
+            vmem((win, 2 * half, 2 * tlen), BF16),
+            vmem((rows, 2 * vectors, 2 * tlen), BF16),
+            vmem((rows, 8, tlen), F32),
             vmem((5, rows, tlen), F32),
             vmem((4, rows, tlen), F32),
             vmem((2, win, vectors, tlen), F32),
@@ -398,7 +437,7 @@
             pltpu.SemaphoreType.DMA((3, 2, most)),
         ],
         compiler_params=pltpu.CompilerParams(
-            collective_id=0, has_side_effects=True, vmem_limit_bytes=48 * 1024 * 1024
+            collective_id=0, has_side_effects=True, vmem_limit_bytes=56 * 1024 * 1024
         ),
     )(table, start_basis, tile_values)
 

time: 89.5 us -> 74.5 us (0.83)
  Pallas kernels: 83.3 us -> 72.7 us
  other arithmetic: 4.33 us -> 0 us
    pallas_call x1, Pallas kernels: 83.3 us -> 69.2 us  [body(): pl.pallas_call(functools.partial(kernel, count, near, slots, rows, vector...]
    pallas_call x0 -> x1, Pallas kernels: none -> 3.47 us  [body(): pl.pallas_call(functools.partial(table_kernel, slots, rows), out_shape=ja...]
    select_n x2 -> x0, other arithmetic: 2.08 us -> none  [the longest x1 1.35 us: body(): place = jnp.where(live, col_here * rows + row_here, -1)]
    reduce_sum x2 -> x0, other arithmetic: 2.06 us -> none  [the longest x1 1.29 us: body(): live = slot < jnp.sum(row_count)]
where the time goes in v2:
time: 74.5 us; the launch traced here: 74.2 us
  Pallas kernels  72.7 us (98%)
  local copies, waits for them, and re-layouts  1.54 us (2%)
    pallas_call x1, Pallas kernels, body(): pl.pallas_call(functools.partial(kernel, count, near, slots, rows, vector...  69.2 us
    pallas_call x1, Pallas kernels, body(): pl.pallas_call(functools.partial(table_kernel, slots, rows), out_shape=ja...  3.47 us
    unnamed x1, local copies, waits for them, and re-layouts  1.54 us

profile of v2, /device:TPU:0, one launch (start us, length us, event | category | flops | bytes accessed | tf_op | source)
XLA Modules:
  0.0 74.2 jit_solution(5591006484035233273)
XLA Ops:
  0.0 3.5 %shard_map.55.tab = s32[832]{0:T(1024)} custom-call(s32[160]{0:T(256)} %tile_row.1, s32[160]{0:T(256)} %tile_col.1, s32[8]{0:T(128)} %row_count.1), custom_call_target="tpu_custom_call" | custom-call | tf_op jit(solution)/shard_map/pallas_call | solution.py:394
  3.5 69.2 %shard_map.56 = f32[24,1024]{1,0:T(8,128)} custom-call(s32[832]{0:T(1024)} %shard_map.55.tab, f32[24,1024]{1,0:T(8,128)} %basis.1, f32[160,128,128]{2,1,0:T(8,128)} %tiles_hbm.1), custom_call_target="tpu_custom_call" | custom-call | tf_op jit(solution)/shard_map/pallas_call | solution.py:404
  72.7 1.5 %copy.7 = f32[24,1024]{1,0:T(8,128)} copy(f32[24,1024]{1,0:T(8,128)} %shard_map.56) | data formatting | bytes 196608

commit v3 on v2

--- a/solution.py
+++ b/solution.py
@@ -102,17 +102,61 @@
             def _(i=i):
                 neighbour(which, i, source, target).wait_recv()
 
-    def own_v(d):
-        return v_win.at[pl.ds(2 * rows, rows)]
-
-    def to_v(d):
-        return v_win.at[pl.ds((2 - d) * rows, rows)]
-
-    def own_v2(d):
-        return v_win2.at[pl.ds(2 * rows, rows)]
-
-    def to_v2(d):
-        return v_win2.at[pl.ds((2 - d) * rows, rows)]
+    core = me % 2
+    mate = me + 1 - 2 * core
+    left_ok, right_ok = valid[0], valid[3]
+    first_core = core == 0
+    second_core = core == 1
+
+    def piece(which, i, source, target, device):
+        return pltpu.make_async_remote_copy(
+            src_ref=source,
+            dst_ref=target,
+            send_sem=x_send.at[which, i],
+            recv_sem=x_recv.at[which, i],
+            device_id={"rows": device},
+            device_id_type=MESH,
+        )
+
+    def halo(which, buf):
+        def block(index):
+            return buf.at[pl.ds(index * rows, rows)]
+
+        down = piece(which, 0, block(2), block(4), me - 2)
+        up = piece(which, 3, block(2), block(0), me + 2)
+        across = piece(which, 1, block(2), block(1 + 2 * core), mate)
+        onward = piece(which, 2, block(4 - 4 * core), block(3 - 2 * core), mate)
+        return down, up, across, onward
+
+    def halo_send(which, buf):
+        down, up, across, _ = halo(which, buf)
+        pl.when(left_ok)(down.start)
+        pl.when(right_ok)(up.start)
+        across.start()
+
+    def halo_finish(which, buf):
+        down, up, across, onward = halo(which, buf)
+
+        @pl.when(jnp.logical_and(first_core, right_ok))
+        def _():
+            down.wait_recv()
+            onward.start()
+
+        @pl.when(jnp.logical_and(second_core, left_ok))
+        def _():
+            up.wait_recv()
+            onward.start()
+
+        pl.when(jnp.logical_and(second_core, right_ok))(down.wait_recv)
+        pl.when(jnp.logical_and(first_core, left_ok))(up.wait_recv)
+        across.wait_send()
+        across.wait_recv()
+        pl.when(left_ok)(down.wait_send)
+        pl.when(right_ok)(up.wait_send)
+        pl.when(jnp.logical_and(first_core, right_ok))(onward.wait_send)
+        pl.when(jnp.logical_and(second_core, left_ok))(onward.wait_send)
+        pl.when(jnp.logical_and(first_core, left_ok))(onward.wait_recv)
+        pl.when(jnp.logical_and(second_core, right_ok))(onward.wait_recv)
 
     def own_s(d):
         return s_win.at[pl.ds(2 * rows, rows)]
@@ -139,7 +183,7 @@
 
     mass_chunk(0)
     pl.semaphore_wait(barrier, greeted)
-    send(0, own_v, to_v)
+    halo_send(0, v_win)
     for c in range(1, chunks):
         mass_chunk(c)
 
@@ -253,7 +297,7 @@
     def forward(step):
         used = 2 * half if step == 0 else 2 * vectors
 
-        @pl.loop(0, slots, unroll=16)
+        @pl.loop(0, slots, unroll=32)
         def _(s):
             left = lhs_win[tab[col_at + s], 0:used]
             both = lax.dot_general(left, t_flip[s], NN, preferred_element_type=F32)
@@ -272,13 +316,13 @@
         return total[0:vectors] * row_inv[r, 0:1]
 
     def backward(step):
-        @pl.loop(0, slots, unroll=16)
+        @pl.loop(0, slots, unroll=32)
         def _(s):
             left = lhs_row[tab[row_at + s]]
             both = lax.dot_general(left, t_own[s], NN, preferred_element_type=F32)
             prod[s, 0:vectors] = both[0:vectors] + both[vectors:]
 
-        @pl.loop(0, win)
+        @pl.loop(0, win, unroll=8)
         def _(c):
             at = cmap_at + c * rows
             total = prod[tab[at], 0:vectors]
@@ -287,24 +331,45 @@
             z_part[step, c] = total
 
     def exchange_z(step):
-        def source(d):
-            return z_part.at[step, pl.ds((2 + d) * rows, rows)]
-
-        def target(d):
-            return z_in.at[step, OFFSETS.index(d)]
-
-        send(3 + step, source, target)
-        finish(3 + step, source, target)
-        z_own[...] = z_part[step, 2 * rows : 3 * rows]
-        for i in range(4):
-            @pl.when(valid[3 - i])
-            def _(i=i):
-                z_own[...] = z_own[...] + z_in[step, i]
+        def window(index):
+            return z_part.at[step, pl.ds(index * rows, rows)]
+
+        which = 3 + step
+        joined = piece(which, 1, window(1 + 2 * core), z_in.at[step, 1], mate)
+        across = piece(which, 2, window(3 - 2 * core), z_in.at[step, 2], mate)
+        down = piece(which, 0, window(0), z_in.at[step, 0], me - 2)
+        up = piece(which, 3, window(4), z_in.at[step, 3], me + 2)
+        joined.start()
+        pl.when(jnp.logical_and(first_core, left_ok))(down.start)
+        pl.when(jnp.logical_and(second_core, right_ok))(up.start)
+        across.start()
+        joined.wait_send()
+        joined.wait_recv()
+        at = pl.ds((4 - 4 * core) * rows, rows)
+        z_part[step, at] = z_part[step, at] + z_in[step, 1]
+        pl.when(jnp.logical_and(first_core, right_ok))(up.start)
+        pl.when(jnp.logical_and(second_core, left_ok))(down.start)
+        across.wait_send()
+        across.wait_recv()
+        z_own[...] = z_part[step, 2 * rows : 3 * rows] + z_in[step, 2]
+
+        @pl.when(right_ok)
+        def _():
+            down.wait_recv()
+            z_own[...] = z_own[...] + z_in[step, 0]
+
+        @pl.when(left_ok)
+        def _():
+            up.wait_recv()
+            z_own[...] = z_own[...] + z_in[step, 3]
+
+        pl.when(left_ok)(down.wait_send)
+        pl.when(right_ok)(up.wait_send)
 
     flip(slots // 2, slots)
     tail = lax.broadcasted_iota(jnp.int32, (16, 2 * tlen), 0)
     ones = jnp.where(tail < 8, 1.0, 0.0).astype(BF16)
-    finish(0, own_v, to_v)
+    halo_finish(0, v_win)
     finish(2, own_s, to_s)
 
     @pl.loop(0, win, unroll=4)
@@ -315,7 +380,7 @@
     forward(0)
     reduce_send(0, 1, reduce_wait(0, 0))
 
-    @pl.loop(0, rows)
+    @pl.loop(0, rows, unroll=4)
     def _(r):
         lhs_row[r] = left_side(row_total(r, 0))
 
@@ -326,9 +391,9 @@
         cleaned = z_own[b] * col_scale[b : b + 1] - along * root[b : b + 1]
         zext[0:vectors, b * tlen : (b + 1) * tlen] = cleaned
         v_win2[2 * rows + b] = cleaned * col_scale[b : b + 1]
-    send(5, own_v2, to_v2)
+    halo_send(5, v_win2)
     reduce_send(1, 0, gram_packed())
-    finish(5, own_v2, to_v2)
+    halo_finish(5, v_win2)
 
     @pl.loop(0, win, unroll=4)
     def _(c):
@@ -338,7 +403,7 @@
     forward(1)
     factor = inverse_factor(*unpack(reduce_wait(1, 1)))
 
-    @pl.loop(0, rows)
+    @pl.loop(0, rows, unroll=4)
     def _(r):
         lhs_row[r] = left_side(mix(factor, row_total(r, 1)))
 

time: 74.5 us -> 65.7 us (0.88)
  Pallas kernels: 72.7 us -> 64 us
    pallas_call x1, Pallas kernels: 69.2 us -> 61 us  [body(): pl.pallas_call(functools.partial(kernel, count, near, slots, rows, vector...]
where the time goes in v3:
time: 65.7 us; the launch traced here: 65.6 us
  Pallas kernels  64 us (97%)
  local copies, waits for them, and re-layouts  1.54 us (2%)
    pallas_call x1, Pallas kernels, body(): pl.pallas_call(functools.partial(kernel, count, near, slots, rows, vector...  61 us
    pallas_call x1, Pallas kernels, body(): pl.pallas_call(functools.partial(table_kernel, slots, rows), out_shape=ja...  3 us
    unnamed x1, local copies, waits for them, and re-layouts  1.54 us

profile of v3, /device:TPU:0, one launch (start us, length us, event | category | flops | bytes accessed | tf_op | source)
XLA Modules:
  0.0 65.6 jit_solution(3072644266176140395)
XLA Ops:
  0.0 3.0 %shard_map.55.tab = s32[832]{0:T(1024)} custom-call(s32[160]{0:T(256)} %tile_row.1, s32[160]{0:T(256)} %tile_col.1, s32[8]{0:T(128)} %row_count.1), custom_call_target="tpu_custom_call" | custom-call | tf_op jit(solution)/shard_map/pallas_call | solution.py:459
  3.0 61.0 %shard_map.56 = f32[24,1024]{1,0:T(8,128)} custom-call(s32[832]{0:T(1024)} %shard_map.55.tab, f32[24,1024]{1,0:T(8,128)} %basis.1, f32[160,128,128]{2,1,0:T(8,128)} %tiles_hbm.1), custom_call_target="tpu_custom_call" | custom-call | tf_op jit(solution)/shard_map/pallas_call | solution.py:469
  64.0 1.5 %copy.7 = f32[24,1024]{1,0:T(8,128)} copy(f32[24,1024]{1,0:T(8,128)} %shard_map.56) | data formatting | bytes 196608

commit v4 on v3

--- a/solution.py
+++ b/solution.py
@@ -134,7 +134,7 @@
         pl.when(right_ok)(up.start)
         across.start()
 
-    def halo_finish(which, buf):
+    def halo_relay(which, buf):
         down, up, across, onward = halo(which, buf)
 
         @pl.when(jnp.logical_and(first_core, right_ok))
@@ -147,6 +147,8 @@
             up.wait_recv()
             onward.start()
 
+    def halo_finish(which, buf):
+        down, up, across, onward = halo(which, buf)
         pl.when(jnp.logical_and(second_core, right_ok))(down.wait_recv)
         pl.when(jnp.logical_and(first_core, left_ok))(up.wait_recv)
         across.wait_send()
@@ -366,6 +368,7 @@
         pl.when(left_ok)(down.wait_send)
         pl.when(right_ok)(up.wait_send)
 
+    halo_relay(0, v_win)
     flip(slots // 2, slots)
     tail = lax.broadcasted_iota(jnp.int32, (16, 2 * tlen), 0)
     ones = jnp.where(tail < 8, 1.0, 0.0).astype(BF16)
@@ -393,13 +396,14 @@
         v_win2[2 * rows + b] = cleaned * col_scale[b : b + 1]
     halo_send(5, v_win2)
     reduce_send(1, 0, gram_packed())
+    halo_relay(5, v_win2)
     halo_finish(5, v_win2)
+    reduce_send(1, 1, reduce_wait(1, 0))
 
     @pl.loop(0, win, unroll=4)
     def _(c):
         lhs_win[c, 0 : 2 * vectors] = left_side(v_win2[c])
 
-    reduce_send(1, 1, reduce_wait(1, 0))
     forward(1)
     factor = inverse_factor(*unpack(reduce_wait(1, 1)))
 
@@ -453,7 +457,7 @@
     rows = row_count.shape[0]
     vectors = start_basis.shape[0]
     count = lax.axis_size("rows")
-    near = 4 if count <= 16 else 8
+    near = count if count <= 16 else 8
     win = 5 * rows
     smem = pl.BlockSpec(memory_space=pltpu.SMEM)
     table = pl.pallas_call(

time: 65.7 us -> 65.1 us (level)
    pallas_call x1, Pallas kernels: 61 us -> 60.1 us  [body(): pl.pallas_call(functools.partial(kernel, count, near, slots, rows, vector...]
where the time goes in v4:
time: 65.1 us; the launch traced here: 64.9 us
  Pallas kernels  63.4 us (97%)
  local copies, waits for them, and re-layouts  1.54 us (2%)
    pallas_call x1, Pallas kernels, body(): pl.pallas_call(functools.partial(kernel, count, near, slots, rows, vector...  60.1 us
    pallas_call x1, Pallas kernels, body(): pl.pallas_call(functools.partial(table_kernel, slots, rows), out_shape=ja...  3.32 us
    unnamed x1, local copies, waits for them, and re-layouts  1.54 us

profile of v4, /device:TPU:0, one launch (start us, length us, event | category | flops | bytes accessed | tf_op | source)
XLA Modules:
  0.0 64.9 jit_solution(16570151910163878838)
XLA Ops:
  0.0 3.3 %shard_map.55.tab = s32[832]{0:T(1024)} custom-call(s32[160]{0:T(256)} %tile_row.1, s32[160]{0:T(256)} %tile_col.1, s32[8]{0:T(128)} %row_count.1), custom_call_target="tpu_custom_call" | custom-call | tf_op jit(solution)/shard_map/pallas_call | solution.py:463
  3.3 60.1 %shard_map.56 = f32[24,1024]{1,0:T(8,128)} custom-call(s32[832]{0:T(1024)} %shard_map.55.tab, f32[24,1024]{1,0:T(8,128)} %basis.1, f32[160,128,128]{2,1,0:T(8,128)} %tiles_hbm.1), custom_call_target="tpu_custom_call" | custom-call | tf_op jit(solution)/shard_map/pallas_call | solution.py:473
  63.4 1.5 %copy.7 = f32[24,1024]{1,0:T(8,128)} copy(f32[24,1024]{1,0:T(8,128)} %shard_map.56) | data formatting | bytes 196608
